TPU v7x, 32 devices: a whole 2x2x4 slice. The times are simulated.
32 devices in a mesh: groups: 2 (over y), feat: 4 (over z), dp: 4 (over x, core).
Axes of the slice: x: 2, y: 2, z: 4, core: 2. Of those that a mesh axis runs over, the one named last changes fastest.
Arguments:
- features: bfloat16 [2048, 8192], P(('groups', 'dp'), 'feat'), parts along dimension 0, may hold values from -6 to 6
- bn_gain: float32 [8192], P('feat'), may hold values from 0.1 to 1.9
- bn_shift: float32 [8192], P('feat'), may hold values from -0.5 to 0.5
- weight: bfloat16 [8192, 8192], P('feat'), may hold values from -2 to 2
Outputs:
- covariance: float32 [16384, 8192], P(('groups', 'dp'), 'feat'), parts along dimension 0
- grad_in: bfloat16 [2048, 8192], P(('groups', 'dp'), 'feat'), parts along dimension 0
There are 2 independent parts, one for each index of `groups`. A program takes and returns all parts, laid end to end along the dimension named above; an argument that names none is the same for every part. Nothing has to cross between parts.
All inputs are finite; a program needn't handle non-finite values.
Results may differ from a plain program's by a relative error of at most 0.014.
Values may be sent and summed in bfloat16 or wider, within the bound.
A program may use at most 256 MiB of HBM per device.

v0:
```python
import jax
import jax.numpy as jnp
from jax import lax
from jax.sharding import PartitionSpec as P


def whole_rows(centered):
    return lax.all_gather(centered, "feat", axis=1, tiled=True)


def shards(features, bn_gain, bn_shift, weight):
    dp_count = lax.axis_size("dp")
    feat_count = lax.axis_size("feat")
    local_rows = features.shape[0]
    images = local_rows * dp_count
    hidden = features.astype(jnp.float32)
    col_sums, col_squares = lax.psum((jnp.sum(hidden, 0), jnp.sum(hidden * hidden, 0)), "dp")
    mean_h = col_sums / images
    var_h = col_squares / images - mean_h * mean_h
    normed = (hidden - mean_h) * lax.rsqrt(var_h + 1e-05) * bn_gain + bn_shift
    activated = jnp.maximum(normed, 0.0).astype(jnp.bfloat16)
    partial_value = jnp.dot(activated, weight, preferred_element_type=jnp.float32)
    projected = lax.psum_scatter(partial_value, "feat", scatter_dimension=1, tiled=True).astype(
        jnp.bfloat16
    )
    proj_f = projected.astype(jnp.float32)
    proj_mean = lax.psum(jnp.sum(proj_f, 0), "dp") / images
    centered = (proj_f - proj_mean).astype(jnp.bfloat16)
    cent_f = centered.astype(jnp.float32)
    width_f = centered.shape[1]
    width_x = width_f * feat_count // dp_count
    cent_full = None
    cent_full = whole_rows(centered)
    cent_x = lax.all_to_all(cent_full, "dp", split_axis=1, concat_axis=0, tiled=True)
    piece = lax.all_gather(centered, "dp", axis=0, tiled=True)
    cov_tile = lax.dot_general(
        cent_x, piece, (((0,), (0,)), ((), ())), preferred_element_type=jnp.float32
    )
    piece_f = piece.astype(jnp.float32)
    cov_tile, sq_sum = (cov_tile, jnp.sum(piece_f * piece_f, 0))
    covariance = cov_tile / (images - 1)
    proj_var = sq_sum / (images - 1)
    spread = jnp.sqrt(proj_var + 0.0001)
    row_ids = lax.axis_index("dp") * width_x + jnp.arange(width_x, dtype=jnp.int32)[:, None]
    col_ids = lax.axis_index("feat") * width_f + jnp.arange(width_f, dtype=jnp.int32)[None, :]
    off_diag = jnp.where(row_ids == col_ids, 0.0, covariance).astype(jnp.bfloat16)
    mixed = jnp.dot(
        cent_full,
        lax.all_gather(off_diag, "dp", axis=0, tiled=True),
        preferred_element_type=jnp.float32,
    )
    scale_up = images / (images - 1)
    active = jnp.where(spread < 1.0, 1.0 / spread, 0.0)
    grad_proj = (4.0 * scale_up * mixed - 25.0 * scale_up * active * cent_f).astype(jnp.bfloat16)
    grad_in = lax.dot_general(
        lax.all_gather(grad_proj, "feat", axis=1, tiled=True),
        weight,
        (((1,), (1,)), ((), ())),
        preferred_element_type=jnp.float32,
    )
    return (covariance, grad_in.astype(jnp.bfloat16))


def solution(mesh):
    in_specs = (P(("groups", "dp"), "feat"), P("feat"), P("feat"), P("feat", None))
    out_specs = (P(("groups", "dp"), "feat"), P(("groups", "dp"), "feat"))
    return jax.shard_map(shards, mesh=mesh, in_specs=in_specs, out_specs=out_specs, check_vma=False)
```

profile of v0, /device:TPU:0, one launch (start us, length us, event | category | flops | bytes accessed | tf_op | source)
XLA Modules:
  0.0 694.4 jit_solution(14080801374418411626)
XLA Ops:
  7.2 0.0 reduce-scatter.2.cloned.1.call-start
  7.2 1.5 convert_reduce_fusion
  8.7 12.7 %all-reduce = (f32[2048]{0:T(1024)S(1)}, f32[2048]{0:T(1024)S(1)}) all-reduce(f32[2048]{0:T(1024)S(1)} %get-tuple-element.3, f32[2048]{0:T(1024)S(1)} %get-tuple-element.2), channel_id=1, replica_groups=mesh['groups'=2,'feat'=4,'dp'=4] {'dp'}, use_global_device_ids=true, to_apply=%region_3.0 | all-reduce | flops 4096 | bytes 32768 | tf_op jit(solution)/shard_map/psum | solution.py:17
  21.4 17.4 %fusion.9 = f32[256,8192]{1,0:T(8,128)} fusion(bf16[2048,8192]{1,0:T(8,128)(2,1)} %param.7, bf16[256,2048]{1,0:T(8,128)(2,1)} %param.4, f32[2048]{0:T(1024)} %param.6, f32[2048]{0:T(1024)} %param.5, f32[2048]{0:T(1024)S(1)} %get-tuple-element.7, f32[2048]{0:T(1024)S(1)} %get-tuple-element.6), kind=kOutput, calls=%fused_computation.20 | convolution fusion | flops 8593604608 | bytes 43024384 | tf_op jit(solution)/shard_map/dot_general | solution.py:22
  38.8 0.0 reduce-scatter.2.cloned.1.call-update
  38.9 0.0 all-gather.5.cloned.1.call-start
  38.9 144.9 %reduce-scatter.2.cloned.1.call-done = f32[256,2048]{1,0:T(8,128)} async-done(((f32[256,8192]{1,0:T(8,128)}), f32[256,2048]{1,0:T(8,128)}) %reduce-scatter.2.cloned.1.call-update) | async-done | bytes 2097168 | tf_op jit(solution)/shard_map/reduce_scatter | solution.py:23
  183.8 1.7 convert_reduce_fusion.1
  185.5 6.5 psum.23
  192.0 2.7 fusion.2
  194.8 0.0 all-gather.5.cloned.1.call-update
  194.8 0.0 all-gather.7.cloned.1.call-start
  194.9 0.7 all-gather.7.cloned.1.call-update
  195.6 80.5 %all-gather.5.cloned.1.call-done = bf16[256,8192]{1,0:T(8,128)(2,1)} async-done(((bf16[256,2048]{1,0:T(8,128)(2,1)}), bf16[256,8192]{1,0:T(8,128)(2,1)}) %all-gather.5.cloned.1.call-update) | async-done | bytes 4194320 | tf_op jit(solution)/shard_map/all_gather | solution.py:8
  276.0 4.8 copy.9
  280.8 4.9 all-to-all-start
  285.8 0.0 all-gather.9.cloned.1.call-start
  285.8 46.1 %all-gather.7.cloned.1.call-done = bf16[1024,2048]{1,0:T(8,128)(2,1)} async-done(((bf16[256,2048]{1,0:T(8,128)(2,1)}), bf16[1024,2048]{1,0:T(8,128)(2,1)}) %all-gather.7.cloned.1.call-update) | async-done | bytes 4194320 | tf_op jit(solution)/shard_map/all_gather | solution.py:35
  332.0 22.7 %all-to-all-done = bf16[256,4,2048]{2,0,1:T(8,128)(2,1)} async-done(((bf16[256,4,2048]{2,0,1:T(8,128)(2,1)}), bf16[256,4,2048]{2,0,1:T(8,128)(2,1)}, u32[]{:S(2)}, u32[]{:S(2)}) %all-to-all-start) | async-done | bytes 4194336 | tf_op jit(solution)/shard_map/all_to_all | solution.py:34
  354.6 17.6 %select_convert_fusion = (bf16[2048,2048]{1,0:T(8,128)(2,1)}, f32[2048,2048]{1,0:T(8,128)}) fusion(s32[2048]{0:T(1024)S(1)} %get-tuple-element.10, s32[2048]{0:T(1024)S(1)} %get-tuple-element.11, bf16[1024,2048]{1,0:T(8,128)(2,1)} %bitcast.1, bf16[1024,2048]{1,0:T(8,128)(2,1)} %all-gather.7.cloned.1.call-done), kind=kOutput, calls=%fused_computation | convolution fusion | flops 8602517504 | bytes 33570816 | tf_op jit(solution)/shard_map/dot_general | solution.py:36
  372.3 0.0 all-gather.9.cloned.1.call-update
  372.3 0.0 copy-start
  372.3 0.2 all-gather.11.cloned.1.call-start
  372.5 3.1 multiply_reduce_fusion
  375.7 197.5 %all-gather.9.cloned.1.call-done = bf16[8192,2048]{1,0:T(8,128)(2,1)} async-done(((bf16[2048,2048]{1,0:T(8,128)(2,1)}), bf16[8192,2048]{1,0:T(8,128)(2,1)}) %all-gather.9.cloned.1.call-update) | async-done | bytes 33554448 | tf_op jit(solution)/shard_map/all_gather | solution.py:49
  573.2 0.0 copy-done
  573.2 17.0 %fusion.1 = bf16[256,2048]{1,0:T(8,128)(2,1)} fusion(bf16[256,8192]{1,0:T(8,128)(2,1)} %all-gather.5.cloned.1.call-done, bf16[8192,2048]{1,0:T(8,128)(2,1)} %all-gather.9.cloned.1.call-done, bf16[256,2048]{1,0:T(8,128)(2,1)S(1)} %copy-done, f32[2048]{0:T(1024)S(1)} %select_multiply_fusion), kind=kOutput, calls=%fused_computation.11 | convolution fusion | flops 8592556032 | bytes 39854080 | tf_op jit(solution)/shard_map/dot_general | solution.py:47
  590.2 0.0 all-gather.11.cloned.1.call-update
  590.3 80.9 %all-gather.11.cloned.1.call-done = bf16[256,8192]{1,0:T(8,128)(2,1)} async-done(((bf16[256,2048]{1,0:T(8,128)(2,1)}), bf16[256,8192]{1,0:T(8,128)(2,1)}) %all-gather.11.cloned.1.call-update) | async-done | bytes 4194320 | tf_op jit(solution)/shard_map/all_gather | solution.py:56
  671.2 16.6 %convolution_convert_fusion = bf16[256,2048]{1,0:T(8,128)(2,1)} fusion(bf16[256,8192]{1,0:T(8,128)(2,1)} %all-gather.11.cloned.1.call-done, bf16[2048,8192]{1,0:T(8,128)(2,1)} %param.7), kind=kOutput, calls=%fused_computation.12 | convolution fusion | flops 8590458880 | bytes 38797312 | tf_op jit(solution)/shard_map/dot_general | solution.py:55
  (4 shorter events, 0.0 us)
Async XLA Ops:
  7.2 176.7 %reduce-scatter.2.cloned.1.call-start = ((), (), s32[]{:S(2)}) async-start(), calls=%async_computation.2 | async-start | bytes 10485760 | tf_op jit(solution)/shard_map/reduce_scatter | solution.py:23
  38.9 237.2 %all-gather.5.cloned.1.call-start = ((), (), s32[]{:S(2)}) async-start(), calls=%async_computation.3 | async-start | bytes 5242880 | tf_op jit(solution)/shard_map/all_gather | solution.py:8
  194.8 137.1 %all-gather.7.cloned.1.call-start = ((), (), s32[]{:S(2)}) async-start(), calls=%async_computation.4 | async-start | bytes 5242880 | tf_op jit(solution)/shard_map/all_gather | solution.py:35
  280.8 73.8 %all-to-all-start = ((bf16[256,4,2048]{2,0,1:T(8,128)(2,1)}), bf16[256,4,2048]{2,0,1:T(8,128)(2,1)}, u32[]{:S(2)}, u32[]{:S(2)}) async-start(bf16[256,4,2048]{2,0,1:T(8,128)(2,1)} %bitcast.14), calls=%async_computation.1 | async-start | bytes 8388608 | tf_op jit(solution)/shard_map/all_to_all | solution.py:34
  285.8 287.4 %all-gather.9.cloned.1.call-start = ((), (), s32[]{:S(2)}) async-start(), calls=%async_computation.5 | async-start | bytes 41943040 | tf_op jit(solution)/shard_map/all_gather | solution.py:49
  372.3 200.9 %copy-start = (bf16[256,2048]{1,0:T(8,128)(2,1)S(1)}, bf16[256,2048]{1,0:T(8,128)(2,1)}, u32[]{:S(2)}) copy-start(bf16[256,2048]{1,0:T(8,128)(2,1)} %fusion.2) | copy-start | bytes 3145732
  372.3 298.9 %all-gather.11.cloned.1.call-start = ((), (), s32[]{:S(2)}) async-start(), calls=%async_computation.6 | async-start | bytes 5242880 | tf_op jit(solution)/shard_map/all_gather | solution.py:56
Sparse Core Ops, SparseCore 0:
  39.0 144.7 reduce-scatter.1
  194.9 81.0 all-gather.4
  278.2 53.7 all-gather.6
  372.4 200.7 all-gather.8
  590.4 80.7 all-gather.10
where the time goes:
time: 695 us; the launch traced here: 694 us
  waiting for transfers between devices  573 us (82%)
  matrix products  68.7 us (10%)
  blocking collectives  19.2 us (3%)
  between operations  13.8 us (2%)
  other arithmetic  9.16 us (1%)
    all_gather x1, waiting for transfers between devices, shards(): lax.all_gather(off_diag, 'dp', axis=0, tiled=True)  198 us
    reduce_scatter x1, waiting for transfers between devices, shards(): lax.psum_scatter(partial_value, 'feat', scatter_dimension=1, tiled=True)  145 us
    all_gather x1, waiting for transfers between devices, shards(): lax.all_gather(grad_proj, 'feat', axis=1, tiled=True)  80.9 us
    all_gather x1, waiting for transfers between devices, whole_rows(): return lax.all_gather(centered, 'feat', axis=1, tiled=True)  80.5 us
    all_gather x1, waiting for transfers between devices, shards(): piece = lax.all_gather(centered, 'dp', axis=0, tiled=True)  46.1 us
    all_to_all x1, waiting for transfers between devices, shards(): lax.all_to_all(cent_full, 'dp', split_axis=1, concat_axis=0, tiled=True)  22.7 us
    dot_general x1, matrix products, shards(): lax.dot_general(cent_x, piece, (((0,), (0,)), ((), ())), preferred_elemen...  17.6 us
    dot_general x1, matrix products, shards(): jnp.dot(activated, weight, preferred_element_type=jnp.float32)  17.4 us
  transfers between devices with their start and end apart: 6, of which 6 were waited for; matrix products, arithmetic and copies ran while one was open for 1% of the time, Pallas kernels for 0%

commit v1 on v0

--- a/solution.py
+++ b/solution.py
@@ -32,7 +32,13 @@
     cent_full = None
     cent_full = whole_rows(centered)
     cent_x = lax.all_to_all(cent_full, "dp", split_axis=1, concat_axis=0, tiled=True)
-    piece = lax.all_gather(centered, "dp", axis=0, tiled=True)
+    size = lax.axis_size("dp")
+    block, parts = (centered, [centered])
+    for _ in range(size - 1):
+        block = lax.ppermute(block, "dp", [(i, (i + 1) % size) for i in range(size)])
+        parts.insert(0, block)
+    flat = jnp.concatenate(parts, axis=0)
+    piece = jnp.roll(flat, (lax.axis_index("dp") + 1) * centered.shape[0], axis=0)
     cov_tile = lax.dot_general(
         cent_x, piece, (((0,), (0,)), ((), ())), preferred_element_type=jnp.float32
     )

time: 695 us -> 673 us (0.968)
  waiting for transfers between devices: 573 us -> 537 us
  local copies, waits for them, and re-layouts: 4.79 us -> 16.4 us
    all_gather x1 -> x0, waiting for transfers between devices: 46.1 us -> none  [shards(): piece = lax.all_gather(centered, 'dp', axis=0, tiled=True)]
    ppermute x0 -> x3, waiting for transfers between devices: none -> 28.8 us  [shards(): lax.ppermute(block, 'dp', [(i, (i + 1) % size) for i in range(size)])]
    all_gather x1, waiting for transfers between devices: 80.5 us -> 52.4 us  [whole_rows(): return lax.all_gather(centered, 'feat', axis=1, tiled=True)]
    unnamed x2 -> x10, local copies, waits for them, and re-layouts: 0.01 us -> 11.6 us
    all_to_all x1, waiting for transfers between devices: 22.7 us -> 34.3 us  [shards(): lax.all_to_all(cent_full, 'dp', split_axis=1, concat_axis=0, tiled=True)]
  transfers between devices with their start and end apart: 6 -> 8, of which waited for: 6 -> 7; matrix products, arithmetic and copies ran while one was open for 1% -> 3% of each run, Pallas kernels for 0% -> 0%
where the time goes in v1:
time: 673 us; the launch traced here: 672 us
  waiting for transfers between devices  537 us (80%)
  matrix products  68.8 us (10%)
  blocking collectives  19.2 us (3%)
  local copies, waits for them, and re-layouts  16.4 us (2%)
  between operations  13.9 us (2%)
  other arithmetic  11.4 us (2%)
    all_gather x1, waiting for transfers between devices, shards(): lax.all_gather(off_diag, 'dp', axis=0, tiled=True)  196 us
    reduce_scatter x1, waiting for transfers between devices, shards(): lax.psum_scatter(partial_value, 'feat', scatter_dimension=1, tiled=True)  145 us
    all_gather x1, waiting for transfers between devices, shards(): lax.all_gather(grad_proj, 'feat', axis=1, tiled=True)  80.9 us
    all_gather x1, waiting for transfers between devices, whole_rows(): return lax.all_gather(centered, 'feat', axis=1, tiled=True)  52.4 us
    all_to_all x1, waiting for transfers between devices, shards(): lax.all_to_all(cent_full, 'dp', split_axis=1, concat_axis=0, tiled=True)  34.3 us
    ppermute x3, waiting for transfers between devices, shards(): lax.ppermute(block, 'dp', [(i, (i + 1) % size) for i in range(size)])  28.8 us
    dot_general x1, matrix products, shards(): lax.dot_general(cent_x, piece, (((0,), (0,)), ((), ())), preferred_elemen...  17.7 us
    dot_general x1, matrix products, shards(): jnp.dot(activated, weight, preferred_element_type=jnp.float32)  17.4 us
  transfers between devices with their start and end apart: 8, of which 7 were waited for; matrix products, arithmetic and copies ran while one was open for 3% of the time, Pallas kernels for 0%

profile of v1, /device:TPU:0, one launch (start us, length us, event | category | flops | bytes accessed | tf_op | source)
XLA Modules:
  0.0 672.1 jit_solution(281793774429425343)
XLA Ops:
  7.2 0.0 reduce-scatter.2.cloned.1.call-start
  7.2 1.5 convert_reduce_fusion
  8.7 12.7 %all-reduce = (f32[2048]{0:T(1024)S(1)}, f32[2048]{0:T(1024)S(1)}) all-reduce(f32[2048]{0:T(1024)S(1)} %get-tuple-element.3, f32[2048]{0:T(1024)S(1)} %get-tuple-element.2), channel_id=1, replica_groups=mesh['groups'=2,'feat'=4,'dp'=4] {'dp'}, use_global_device_ids=true, to_apply=%region_3.0 | all-reduce | flops 4096 | bytes 32768 | tf_op jit(solution)/shard_map/psum | solution.py:17
  21.4 17.4 %fusion.10 = f32[256,8192]{1,0:T(8,128)} fusion(bf16[2048,8192]{1,0:T(8,128)(2,1)} %param.7, bf16[256,2048]{1,0:T(8,128)(2,1)} %param.4, f32[2048]{0:T(1024)} %param.6, f32[2048]{0:T(1024)} %param.5, f32[2048]{0:T(1024)S(1)} %get-tuple-element.7, f32[2048]{0:T(1024)S(1)} %get-tuple-element.6), kind=kOutput, calls=%fused_computation.21 | convolution fusion | flops 8593604608 | bytes 43024384 | tf_op jit(solution)/shard_map/dot_general | solution.py:22
  38.8 0.0 reduce-scatter.2.cloned.1.call-update
  38.9 0.0 all-gather.4.cloned.1.call-start
  38.9 144.9 %reduce-scatter.2.cloned.1.call-done = f32[256,2048]{1,0:T(8,128)} async-done(((f32[256,8192]{1,0:T(8,128)}), f32[256,2048]{1,0:T(8,128)}) %reduce-scatter.2.cloned.1.call-update) | async-done | bytes 2097168 | tf_op jit(solution)/shard_map/reduce_scatter | solution.py:23
  183.8 1.7 convert_reduce_fusion.1
  185.5 6.5 psum.23
  192.0 2.7 fusion.3
  194.8 0.0 all-gather.4.cloned.1.call-update
  194.8 0.1 collective-permute-start
  194.9 14.4 %collective-permute-done = bf16[256,2048]{1,0:T(8,128)(2,1)S(1)} collective-permute-done((bf16[256,2048]{1,0:T(8,128)(2,1)}, bf16[256,2048]{1,0:T(8,128)(2,1)S(1)}, u32[]{:S(2)}, u32[]{:S(2)}) %collective-permute-start) | collective-permute-done | bytes 1048608 | tf_op jit(solution)/shard_map/ppermute | solution.py:38
  209.3 0.0 collective-permute-start.1
  209.3 14.3 %collective-permute-done.1 = bf16[256,2048]{1,0:T(8,128)(2,1)} collective-permute-done((bf16[256,2048]{1,0:T(8,128)(2,1)S(1)}, bf16[256,2048]{1,0:T(8,128)(2,1)}, u32[]{:S(2)}, u32[]{:S(2)}) %collective-permute-start.1) | collective-permute-done | bytes 1048608 | tf_op jit(solution)/shard_map/ppermute | solution.py:38
  223.6 0.0 collective-permute-start.2
  223.6 52.4 %all-gather.4.cloned.1.call-done = bf16[256,8192]{1,0:T(8,128)(2,1)} async-done(((bf16[256,2048]{1,0:T(8,128)(2,1)}), bf16[256,8192]{1,0:T(8,128)(2,1)}) %all-gather.4.cloned.1.call-update) | async-done | bytes 4194320 | tf_op jit(solution)/shard_map/all_gather | solution.py:8
  276.0 4.8 copy.9
  280.8 4.8 all-to-all-start
  285.7 0.0 copy-start
  285.7 0.0 all-gather.6.cloned.1.call-start
  285.7 0.0 collective-permute-done.2
  285.8 2.4 constant_dynamic-update-slice_fusion.7
  288.2 2.4 constant_dynamic-update-slice_fusion.6
  290.6 1.1 constant_dynamic-update-slice_fusion.5
  291.6 0.0 copy-done
  291.6 1.1 constant_dynamic-update-slice_fusion.4
  292.8 2.3 constant_dynamic-update-slice_fusion.3
  295.1 2.3 constant_dynamic-update-slice_fusion.2
  297.4 1.1 constant_dynamic-update-slice_fusion.1
  298.5 1.1 constant_dynamic-update-slice_fusion
  299.6 34.3 %all-to-all-done = bf16[256,4,2048]{2,0,1:T(8,128)(2,1)} async-done(((bf16[256,4,2048]{2,0,1:T(8,128)(2,1)}), bf16[256,4,2048]{2,0,1:T(8,128)(2,1)}, u32[]{:S(2)}, u32[]{:S(2)}) %all-to-all-start) | async-done | bytes 4194336 | tf_op jit(solution)/shard_map/all_to_all | solution.py:34
  333.9 17.7 %select_convert_fusion = (bf16[2048,2048]{1,0:T(8,128)(2,1)}, f32[2048,2048]{1,0:T(8,128)}) fusion(s32[2048]{0:T(1024)S(1)} %get-tuple-element.10, s32[2048]{0:T(1024)S(1)} %get-tuple-element.11, bf16[1024,2048]{1,0:T(8,128)(2,1)} %bitcast.1, bf16[2048,2048]{1,0:T(8,128)(2,1)} %constant_dynamic-update-slice_fusion, s32[]{:T(128)S(6)} %select_n.26), kind=kOutput, calls=%fused_computation | convolution fusion | flops 8602517504 | bytes 33570820 | tf_op jit(solution)/shard_map/dot_general | solution.py:42
  351.6 0.0 all-gather.6.cloned.1.call-update
  351.6 0.0 copy-start.1
  351.6 0.2 all-gather.8.cloned.1.call-start
  351.8 3.1 multiply_reduce_fusion
  355.0 195.9 %all-gather.6.cloned.1.call-done = bf16[8192,2048]{1,0:T(8,128)(2,1)} async-done(((bf16[2048,2048]{1,0:T(8,128)(2,1)}), bf16[8192,2048]{1,0:T(8,128)(2,1)}) %all-gather.6.cloned.1.call-update) | async-done | bytes 33554448 | tf_op jit(solution)/shard_map/all_gather | solution.py:55
  550.9 0.0 copy-done.1
  550.9 17.0 %fusion.2 = bf16[256,2048]{1,0:T(8,128)(2,1)} fusion(bf16[256,8192]{1,0:T(8,128)(2,1)} %all-gather.4.cloned.1.call-done, bf16[8192,2048]{1,0:T(8,128)(2,1)} %all-gather.6.cloned.1.call-done, bf16[256,2048]{1,0:T(8,128)(2,1)S(1)} %copy-done.1, f32[2048]{0:T(1024)S(1)} %select_multiply_fusion), kind=kOutput, calls=%fused_computation.12 | convolution fusion | flops 8592556032 | bytes 39854080 | tf_op jit(solution)/shard_map/dot_general | solution.py:53
  567.9 0.0 all-gather.8.cloned.1.call-update
  568.0 80.9 %all-gather.8.cloned.1.call-done = bf16[256,8192]{1,0:T(8,128)(2,1)} async-done(((bf16[256,2048]{1,0:T(8,128)(2,1)}), bf16[256,8192]{1,0:T(8,128)(2,1)}) %all-gather.8.cloned.1.call-update) | async-done | bytes 4194320 | tf_op jit(solution)/shard_map/all_gather | solution.py:62
  648.9 16.6 %convolution_convert_fusion = bf16[256,2048]{1,0:T(8,128)(2,1)} fusion(bf16[256,8192]{1,0:T(8,128)(2,1)} %all-gather.8.cloned.1.call-done, bf16[2048,8192]{1,0:T(8,128)(2,1)} %param.7), kind=kOutput, calls=%fused_computation.13 | convolution fusion | flops 8590458880 | bytes 38797312 | tf_op jit(solution)/shard_map/dot_general | solution.py:61
  (4 shorter events, 0.0 us)
Async XLA Ops:
  7.2 176.7 %reduce-scatter.2.cloned.1.call-start = ((), (), s32[]{:S(2)}) async-start(), calls=%async_computation.2 | async-start | bytes 10485760 | tf_op jit(solution)/shard_map/reduce_scatter | solution.py:23
  38.9 237.2 %all-gather.4.cloned.1.call-start = ((), (), s32[]{:S(2)}) async-start(), calls=%async_computation.3 | async-start | bytes 5242880 | tf_op jit(solution)/shard_map/all_gather | solution.py:8
  194.8 14.5 %collective-permute-start = (bf16[256,2048]{1,0:T(8,128)(2,1)}, bf16[256,2048]{1,0:T(8,128)(2,1)S(1)}, u32[]{:S(2)}, u32[]{:S(2)}) collective-permute-start(bf16[256,2048]{1,0:T(8,128)(2,1)} %fusion.3), channel_id=1, source_target_pairs={{0,1},{1,2},{2,3},{3,0},{4,5},{5,6},{6,7},{7,4},{8,9},{9,10},{10,1... | collective-permute-start | bytes 3145736 | tf_op jit(solution)/shard_map/ppermute | solution.py:38
  209.3 14.3 %collective-permute-start.1 = (bf16[256,2048]{1,0:T(8,128)(2,1)S(1)}, bf16[256,2048]{1,0:T(8,128)(2,1)}, u32[]{:S(2)}, u32[]{:S(2)}) collective-permute-start(bf16[256,2048]{1,0:T(8,128)(2,1)S(1)} %collective-permute-done), channel_id=1, source_target_pairs={{0,1},{1,2},{2,3},{3,0},{4,5},{5,6},{6,7},{7,4},{8,9},{9,10},{10,1... | collective-permute-start | bytes 3145736 | tf_op jit(solution)/shard_map/ppermute | solution.py:38
  223.6 62.1 %collective-permute-start.2 = (bf16[256,2048]{1,0:T(8,128)(2,1)}, bf16[256,2048]{1,0:T(8,128)(2,1)}, u32[]{:S(2)}, u32[]{:S(2)}) collective-permute-start(bf16[256,2048]{1,0:T(8,128)(2,1)} %collective-permute-done.1), channel_id=1, source_target_pairs={{0,1},{1,2},{2,3},{3,0},{4,5},{5,6},{6,7},{7,4},{8,9},{9,10},{10,1... | collective-permute-start | bytes 3145736 | tf_op jit(solution)/shard_map/ppermute | solution.py:38
  280.8 53.1 %all-to-all-start = ((bf16[256,4,2048]{2,0,1:T(8,128)(2,1)}), bf16[256,4,2048]{2,0,1:T(8,128)(2,1)}, u32[]{:S(2)}, u32[]{:S(2)}) async-start(bf16[256,4,2048]{2,0,1:T(8,128)(2,1)} %bitcast.13), calls=%async_computation.1 | async-start | bytes 8388608 | tf_op jit(solution)/shard_map/all_to_all | solution.py:34
  285.7 6.0 copy-start
  285.7 265.2 %all-gather.6.cloned.1.call-start = ((), (), s32[]{:S(2)}) async-start(), calls=%async_computation.4 | async-start | bytes 41943040 | tf_op jit(solution)/shard_map/all_gather | solution.py:55
  351.6 199.3 %copy-start.1 = (bf16[256,2048]{1,0:T(8,128)(2,1)S(1)}, bf16[256,2048]{1,0:T(8,128)(2,1)}, u32[]{:S(2)}) copy-start(bf16[256,2048]{1,0:T(8,128)(2,1)} %fusion.3) | copy-start | bytes 3145732
  351.6 297.3 %all-gather.8.cloned.1.call-start = ((), (), s32[]{:S(2)}) async-start(), calls=%async_computation.5 | async-start | bytes 5242880 | tf_op jit(solution)/shard_map/all_gather | solution.py:62
Sparse Core Ops, SparseCore 0:
  39.0 144.7 reduce-scatter.1
  194.9 81.0 all-gather.3
  351.7 199.1 all-gather.5
  568.1 80.7 all-gather.7
